TPU v7x, 32 devices: a whole 2x2x4 slice. The times are simulated.
32 devices in a mesh: grp: 2 (over y), seq: 16 (over z, x, core).
Axes of the slice: x: 2, y: 2, z: 4, core: 2. Of those that a mesh axis runs over, the one named last changes fastest.
Arguments:
- normed_input: bfloat16 [4096, 8192], P(('grp', 'seq')), parts along dimension 0, may hold values from -6 to 6
- base_projection_weight: bfloat16 [4096, 1280], P(('grp', 'seq')), parts along dimension 0, may hold values from -24 to 24
- adapter_down_pool: bfloat16 [16, 192, 8192], P('seq'), may hold values from -0.0625 to 0.0625
- adapter_up_pool: bfloat16 [16, 64, 1280], P('seq'), may hold values from -0.75 to 0.75
- output_down_pool: bfloat16 [16, 64, 1024], P('seq'), may hold values from -0.1875 to 0.1875
- output_up_pool: bfloat16 [16, 64, 8192], P('seq'), may hold values from -0.75 to 0.75
- request_adapter_ids: int32 [4], P('grp'), parts along dimension 0, may hold values from 0 to 15, as said below
- holder: int32 [16], replicated, may hold values from 0 to 15, each once
- segment_adapter_entry: int32 [32], P(('grp', 'seq')), parts along dimension 0, may hold values from 0 to 1
Outputs:
- attended: bfloat16 [4096, 1024], P(('grp', 'seq')), parts along dimension 0
- output_delta: bfloat16 [4096, 8192], P(('grp', 'seq')), parts along dimension 0
There are 2 independent parts, one for each index of `grp`. A program takes and returns all parts, laid end to end along the dimension named above; an argument that names none is the same for every part. Nothing has to cross between parts.
Inputs may be any that keep to these rules, and one draw needn't show every extreme that they name: `request_adapter_ids`: 2 distinct adapter ids; the largest is 15.
All inputs are finite; a program needn't handle non-finite values.
Results may differ from a plain program's by a relative error of at most 0.012.
The roundings to bfloat16 on the way count: a program that leaves them out, or rounds other values in their place, can miss the bound.
Values may be sent and summed in bfloat16 or wider, within the bound.
A program may use at most 64 MiB of HBM per device.

v0:
```python
from functools import partial
import math

import jax
import jax.numpy as jnp
from jax import lax
from jax.sharding import PartitionSpec as P

HEAD_SIZE = 128
QUERY_PER_GROUP = 8
ADAPTER_RANK = 64
USED = 2


rope_base = 1000000.0


def spread(value, axis, source):
    kept = jnp.where(lax.axis_index(axis) == source, value, 0).astype(value.dtype)
    return lax.psum(kept, axis)


def rope_tables(positions, head_width):
    half_width = head_width // 2
    frequency = jnp.exp(
        jnp.arange(half_width, dtype=jnp.float32) * (-2.0 * math.log(rope_base) / head_width)
    )
    angles = positions.astype(jnp.float32)[:, None] * frequency[None, :]
    return (jnp.cos(angles), jnp.sin(angles))


def rotate(vectors, cosine, sine_table):
    half_width = vectors.shape[-1] // 2
    first_half = vectors[..., :half_width]
    second_half = vectors[..., half_width:]
    return jnp.concatenate(
        [
            first_half * cosine - second_half * sine_table,
            second_half * cosine + first_half * sine_table,
        ],
        -1,
    )


def absorb(states, queries, positions, key_block, value_block, key_start):
    maxima, totals, summed = states
    scores = jnp.einsum(
        "qhd,kd->hqk", queries, key_block, preferred_element_type=jnp.float32
    ) * HEAD_SIZE ** (-0.5)
    visible = (key_start + jnp.arange(key_block.shape[0], dtype=jnp.int32))[None, :] <= positions[
        :, None
    ]
    scores = jnp.where(visible[None], scores, -1e30)
    new_maxima = jnp.maximum(maxima, jnp.max(scores, -1))
    weights = jnp.where(visible[None], jnp.exp(scores - new_maxima[:, :, None]), 0.0)
    rescale = jnp.exp(maxima - new_maxima)
    totals = totals * rescale + jnp.sum(weights, -1)
    summed = summed * rescale[:, :, None] + jnp.einsum(
        "hqk,kd->hqd", weights.astype(jnp.bfloat16), value_block, preferred_element_type=jnp.float32
    )
    return (new_maxima, totals, summed)


def keep_state(states):
    return states


def pick_slot(stacked, adapter_pick):
    return lax.dynamic_index_in_dim(stacked, adapter_pick, 0, keepdims=False)


def shards(
    normed_input,
    base_projection_weight,
    adapter_down_pool,
    adapter_up_pool,
    output_down_pool,
    output_up_pool,
    request_adapter_ids,
    holder,
    segment_adapter_entry,
):
    tok_rows = normed_input.shape[0]
    query_width = QUERY_PER_GROUP * HEAD_SIZE
    fetched = []
    for adapter_number in range(USED):
        owning_device = holder[request_adapter_ids[adapter_number]]
        fetched.append(
            (
                spread(adapter_down_pool[0], "seq", owning_device),
                spread(adapter_up_pool[0], "seq", owning_device),
                spread(output_down_pool[0], "seq", owning_device),
                spread(output_up_pool[0], "seq", owning_device),
            )
        )
    stacked_in = [
        jnp.stack([fetched_set[member] for fetched_set in fetched]) for member in range(2)
    ]
    stacked_out = [
        jnp.stack([fetched_set[member] for fetched_set in fetched]) for member in range(2, 4)
    ]
    segment = 0
    adapter_pick = segment_adapter_entry[segment]
    down_weight = pick_slot(stacked_in[0], adapter_pick)
    up_weight = pick_slot(stacked_in[1], adapter_pick)
    reduced_rank_rows = lax.dot_general(
        normed_input, down_weight, (((1,), (1,)), ((), ())), preferred_element_type=jnp.float32
    ).astype(jnp.bfloat16)
    delta_query = jnp.dot(
        reduced_rank_rows[:, :ADAPTER_RANK],
        up_weight[:, :query_width],
        preferred_element_type=jnp.float32,
    )
    delta_key = jnp.dot(
        reduced_rank_rows[:, ADAPTER_RANK : 2 * ADAPTER_RANK],
        up_weight[:, query_width : query_width + HEAD_SIZE],
        preferred_element_type=jnp.float32,
    )
    delta_value = jnp.dot(
        reduced_rank_rows[:, 2 * ADAPTER_RANK :],
        up_weight[:, query_width + HEAD_SIZE :],
        preferred_element_type=jnp.float32,
    )
    deltas = jnp.concatenate([delta_query, delta_key, delta_value], 1)
    combined = base_projection_weight.astype(jnp.float32) + deltas
    device_index = lax.axis_index("seq")
    positions = device_index * tok_rows + jnp.arange(tok_rows, dtype=jnp.int32)
    cosine, sine_table = rope_tables(positions, HEAD_SIZE)
    queries = rotate(
        combined[:, :query_width].reshape(tok_rows, QUERY_PER_GROUP, HEAD_SIZE),
        cosine[:, None, :],
        sine_table[:, None, :],
    ).astype(jnp.bfloat16)
    key_rows = rotate(
        combined[:, query_width : query_width + HEAD_SIZE], cosine, sine_table
    ).astype(jnp.bfloat16)
    value_rows = combined[:, query_width + HEAD_SIZE :].astype(jnp.bfloat16)
    groups = [(queries, positions)]
    initial = tuple(
        (
            (
                jnp.full((QUERY_PER_GROUP, group_pair[0].shape[0]), -1e30, jnp.float32),
                jnp.zeros((QUERY_PER_GROUP, group_pair[0].shape[0]), jnp.float32),
                jnp.zeros((QUERY_PER_GROUP, group_pair[0].shape[0], HEAD_SIZE), jnp.float32),
            )
            for group_pair in groups
        )
    )
    key_piece = lax.all_gather(key_rows, "seq", axis=0, tiled=True)
    value_piece = lax.all_gather(value_rows, "seq", axis=0, tiled=True)
    piece_rows = key_piece.shape[0]
    block_rows = math.gcd(piece_rows, 512)

    def one_block(block_index, states):
        local_start = block_index * block_rows
        key_block = lax.dynamic_slice_in_dim(key_piece, local_start, block_rows, 0)
        value_block = lax.dynamic_slice_in_dim(value_piece, local_start, block_rows, 0)
        updated = []
        for group_pair, group_state in zip(groups, states):
            group_queries, group_positions = group_pair
            updated.append(
                lax.cond(
                    local_start <= group_positions[-1],
                    partial(
                        absorb,
                        queries=group_queries,
                        positions=group_positions,
                        key_block=key_block,
                        value_block=value_block,
                        key_start=local_start,
                    ),
                    keep_state,
                    group_state,
                )
            )
        return tuple(updated)

    results = lax.fori_loop(0, piece_rows // block_rows, one_block, initial)
    outputs = []
    for group_result in results:
        maxima, totals, summed = group_result
        normalized = (summed / totals[:, :, None]).transpose(1, 0, 2)
        outputs.append(normalized.reshape(normalized.shape[0], query_width).astype(jnp.bfloat16))
    attended = outputs[0]
    segment = 0
    adapter_pick = segment_adapter_entry[segment]
    out_down = pick_slot(stacked_out[0], adapter_pick)
    out_up = pick_slot(stacked_out[1], adapter_pick)
    reduced_rank_rows = lax.dot_general(
        attended, out_down, (((1,), (1,)), ((), ())), preferred_element_type=jnp.float32
    ).astype(jnp.bfloat16)
    out_rows = jnp.dot(reduced_rank_rows, out_up, preferred_element_type=jnp.float32).astype(
        jnp.bfloat16
    )
    return (attended, out_rows)


def solution(mesh):
    in_specs = (
        P(("grp", "seq"), None),
        P(("grp", "seq"), None),
        P("seq", None, None),
        P("seq", None, None),
        P("seq", None, None),
        P("seq", None, None),
        P("grp"),
        P(),
        P(("grp", "seq")),
    )
    out_specs = (P(("grp", "seq"), None), P(("grp", "seq"), None))
    return jax.shard_map(shards, mesh=mesh, in_specs=in_specs, out_specs=out_specs, check_vma=False)
```

profile of v0, /device:TPU:27, one launch (start us, length us, event | category | flops | bytes accessed | tf_op | source)
XLA Modules:
  0.0 279.5 jit_solution(13151024051911576124)
XLA Ops:
  7.2 1.4 fusion.56
  12.5 1.3 fusion.55
  15.1 5.0 %broadcast_select_fusion = (bf16[1,192,8192]{2,1,0:T(8,128)(2,1)}, bf16[1,192,8192]{2,1,0:T(8,128)(2,1)}) fusion(bf16[1,192,8192]{2,1,0:T(8,128)(2,1)} %param.15, pred[]{:T(512)S(6)} %eq.5, pred[]{:T(512)S(6)} %eq.4), kind=kLoop, calls=%fused_computation.30 | loop fusion | flops 3145728 | bytes 9437186 | tf_op jit(solution)/shard_map/jit(_where)/select_n | solution.py:19
  20.2 1.5 broadcast_select_fusion.2
  21.6 0.7 broadcast_select_fusion.4
  22.4 0.7 broadcast_select_fusion.6
  23.8 180.8 %all-reduce.3.cloned.1.call-done = (bf16[1,64,1280]{2,1,0:T(8,128)(2,1)}, bf16[1,64,1280]{2,1,0:T(8,128)(2,1)}, bf16[1,192,8192]{2,1,0:T(8,128)(2,1)}, bf16[1,19...) async-done(((bf16[1,64,1280]{2,1,0:T(8,128)(2,1)}, ...) | async-done | bytes 8978448 | tf_op jit(solution)/shard_map/psum | solution.py:20
  204.7 1.0 fusion.33
  205.7 3.4 %fusion.25 = bf16[128,192]{0,1:T(8,128)(2,1)S(1)} fusion(bf16[128,8192]{1,0:T(8,128)(2,1)S(1)} %copy-done, s32[]{:T(128)S(6)} %select_n.127, bf16[1,192,8192]{2,1,0:T(8,128)(2,1)} %get-tuple-element.275, bf16[1,192,8192]{2,1,0:T(8,128)(2,1)} %get-tuple-element.276), kind=kOutput, calls=%fused_computation.35 | convolution fusion | flops 404250624 | bytes 8437764 | tf_op jit(solution)/shard_map/dot_general | solution.py:106
  209.1 0.2 fusion.38
  209.3 0.2 fusion.43
  209.5 0.2 fusion.40
  209.7 0.1 maximum_add_fusion
  209.8 0.1 copy.23
  209.9 0.2 fusion.54
  210.1 0.3 multiply_cosine_fusion
  210.5 0.1 pad_maximum_fusion.1
  210.6 17.9 %all_gather.6 = bf16[2048,128]{1,0:T(8,128)(2,1)S(1)} all-gather(bf16[128,128]{1,0:T(8,128)(2,1)S(1)} %pad_maximum_fusion.1), channel_id=1, replica_groups=mesh['grp'=2,'seq'=16] {'seq'}, dimensions={0}, use_global_device_ids=true | all-gather | bytes 557056 | tf_op jit(solution)/shard_map/all_gather | solution.py:149
  228.5 23.1 %all_gather.7 = bf16[2048,128]{1,0:T(8,128)(2,1)} all-gather(bf16[128,128]{1,0:T(8,128)(2,1)S(1)} %slice.97), channel_id=1, replica_groups=mesh['grp'=2,'seq'=16] {'seq'}, dimensions={0}, use_global_device_ids=true | all-gather | bytes 557056 | tf_op jit(solution)/shard_map/all_gather | solution.py:150
  251.5 0.2 subtract_convert_fusion
  251.7 0.1 pad_maximum_fusion
  252.0 16.8 %while.17 = (s32[]{:T(128)}, f32[8,128]{1,0:T(8,128)S(1)}, f32[8,128]{1,0:T(8,128)S(1)}, f32[8,128,128]{2,1,0:T(8,128)S(1)}, s32[128]{0:T(128)S(1)}, /*index=5*/...) while((s32[]{:T(128)}, f32[8,128]{1,0:T(8,128)S(1)}, ...), condition=%wide.region_9.10_spmd, body=%wide.region_4.0_spmd.sunk | while | flops 275581440 | bytes 8196909 | solution.py:178
  252.0 0.6 slice.103
  253.2 2.9 %conditional.2 = ((f32[8,128]{1,0:T(8,128)S(1)}, f32[8,128]{1,0:T(8,128)S(1)}, f32[8,128,128]{2,1,0:T(8,128)S(1)})) conditional(s32[]{:T(128)} %convert_element_type.86, (f32[8,128]{1,0:T(8,128)S(1)}, f32[8,128]{1,0:T(8,128)S(1)}, f32[8,128,128]{2,1,0:T(8,128)S(1)}) %tuple.64, (s32[]{:T(128)}, s32[128]{0:T(128)S(1)}, bf16[2048,128]{1,0:T(8,128)(2,1)S(1)}, ...), branch_computations={%region_5.5_spmd, %region_6.8_spmd} | conditional | flops 275581440 | bytes 8196686 | solution.py:162
  253.2 0.1 broadcast_compare_fusion
  253.4 0.5 fusion
  253.9 0.5 fusion.2
  254.4 1.7 convolution_add_fusion
  256.2 0.6 slice.103
  257.4 2.9 %conditional.2 = ((f32[8,128]{1,0:T(8,128)S(1)}, f32[8,128]{1,0:T(8,128)S(1)}, f32[8,128,128]{2,1,0:T(8,128)S(1)})) conditional(s32[]{:T(128)} %convert_element_type.86, (f32[8,128]{1,0:T(8,128)S(1)}, f32[8,128]{1,0:T(8,128)S(1)}, f32[8,128,128]{2,1,0:T(8,128)S(1)}) %tuple.64, (s32[]{:T(128)}, s32[128]{0:T(128)S(1)}, bf16[2048,128]{1,0:T(8,128)(2,1)S(1)}, ...), branch_computations={%region_5.5_spmd, %region_6.8_spmd} | conditional | flops 275581440 | bytes 8196686 | solution.py:162
  257.4 0.1 broadcast_compare_fusion
  257.6 0.5 fusion
  258.1 0.5 fusion.2
  258.6 1.7 convolution_add_fusion
  260.4 0.6 slice.103
  261.6 2.9 %conditional.2 = ((f32[8,128]{1,0:T(8,128)S(1)}, f32[8,128]{1,0:T(8,128)S(1)}, f32[8,128,128]{2,1,0:T(8,128)S(1)})) conditional(s32[]{:T(128)} %convert_element_type.86, (f32[8,128]{1,0:T(8,128)S(1)}, f32[8,128]{1,0:T(8,128)S(1)}, f32[8,128,128]{2,1,0:T(8,128)S(1)}) %tuple.64, (s32[]{:T(128)}, s32[128]{0:T(128)S(1)}, bf16[2048,128]{1,0:T(8,128)(2,1)S(1)}, ...), branch_computations={%region_5.5_spmd, %region_6.8_spmd} | conditional | flops 275581440 | bytes 8196686 | solution.py:162
  261.6 0.1 broadcast_compare_fusion
  261.8 0.5 fusion
  262.3 0.5 fusion.2
  262.8 1.7 convolution_add_fusion
  264.6 0.6 slice.103
  265.8 2.9 %conditional.2 = ((f32[8,128]{1,0:T(8,128)S(1)}, f32[8,128]{1,0:T(8,128)S(1)}, f32[8,128,128]{2,1,0:T(8,128)S(1)})) conditional(s32[]{:T(128)} %convert_element_type.86, (f32[8,128]{1,0:T(8,128)S(1)}, f32[8,128]{1,0:T(8,128)S(1)}, f32[8,128,128]{2,1,0:T(8,128)S(1)}) %tuple.64, (s32[]{:T(128)}, s32[128]{0:T(128)S(1)}, bf16[2048,128]{1,0:T(8,128)(2,1)S(1)}, ...), branch_computations={%region_5.5_spmd, %region_6.8_spmd} | conditional | flops 275581440 | bytes 8196686 | solution.py:162
  265.8 0.1 broadcast_compare_fusion
  266.0 0.5 fusion
  266.5 0.5 fusion.2
  267.0 1.7 convolution_add_fusion
  268.8 0.2 copy_bitcast_fusion
  269.0 3.7 %convolution_convert_fusion = bf16[128,8192]{1,0:T(8,128)(2,1)} fusion(bf16[128,1024]{1,0:T(8,128)(2,1)S(1)} %copy_bitcast_fusion, s32[]{:T(128)S(6)} %select_n.127, bf16[1,64,8192]{2,1,0:T(8,128)(2,1)} %get-tuple-element.277, bf16[1,64,8192]{2,1,0:T(8,128)(2,1)} %get-tuple-element.278, bf16[1,64,1024]{2,1,0:T(8,128)(2,1)S(1)} %copy-done.6, ...), kind=kOutput, calls=%fused_computation.24 | convolution fusion | flops 152641536 | bytes 4719616 | tf_op jit(solution)/shard_map/dot_general | solution.py:192
  (40 shorter events, 0.3 us)
Async XLA Ops:
  7.2 198.5 %copy-start = (bf16[128,8192]{1,0:T(8,128)(2,1)S(1)}, bf16[128,8192]{1,0:T(8,128)(2,1)}, u32[]{:S(2)}) copy-start(bf16[128,8192]{1,0:T(8,128)(2,1)} %param.13) | copy-start | bytes 6291460
  7.2 197.5 %all-reduce.3.cloned.1.call-start = ((), (), s32[]{:S(2)}) async-start(), calls=%async_computation | async-start | bytes 17956864 | tf_op jit(solution)/shard_map/psum | solution.py:20
  15.1 5.0 %copy-start.2 = (bf16[1,64,8192]{2,1,0:T(8,128)(2,1)S(1)}, bf16[1,64,8192]{2,1,0:T(8,128)(2,1)}, u32[]{:S(2)}) copy-start(bf16[1,64,8192]{2,1,0:T(8,128)(2,1)} %param.18) | copy-start | bytes 3145732
  20.2 1.5 copy-start.4
  20.2 2.2 copy-start.5
  205.7 4.0 %copy-start.3 = (bf16[128,1280]{1,0:T(8,128)(2,1)S(1)}, bf16[128,1280]{1,0:T(8,128)(2,1)}, u32[]{:S(2)}) copy-start(bf16[128,1280]{1,0:T(8,128)(2,1)} %param.14) | copy-start | bytes 983044
  251.9 17.1 %copy-start.6 = (bf16[1,64,1024]{2,1,0:T(8,128)(2,1)S(1)}, bf16[1,64,1024]{2,1,0:T(8,128)(2,1)}, u32[]{:S(2)}) copy-start(bf16[1,64,1024]{2,1,0:T(8,128)(2,1)} %get-tuple-element.279) | copy-start | bytes 393220
  269.0 3.7 %copy-start.1 = (bf16[128,1024]{1,0:T(8,128)(2,1)}, bf16[128,1024]{1,0:T(8,128)(2,1)S(1)}, u32[]{:S(2)}) copy-start(bf16[128,1024]{1,0:T(8,128)(2,1)S(1)} %copy_bitcast_fusion) | copy-start | bytes 786436
Sparse Core Ops, SparseCore 0:
  23.3 181.3 all-reduce.2
where the time goes:
time: 280 us
  waiting for transfers between devices  181 us (65%)
  blocking collectives  41 us (15%)
  between operations  20.1 us (7%)
  matrix products  16.4 us (6%)
  other arithmetic  12.6 us (4%)
  local copies, waits for them, and re-layouts  5.49 us (2%)
  loops' own time  3.03 us (1%)
    psum x1, waiting for transfers between devices, spread(): return lax.psum(kept, axis)  181 us
    all_gather x1, blocking collectives, shards(): value_piece = lax.all_gather(value_rows, 'seq', axis=0, tiled=True)  23.1 us
    all_gather x1, blocking collectives, shards(): key_piece = lax.all_gather(key_rows, 'seq', axis=0, tiled=True)  17.9 us
    select_n x4, other arithmetic, spread(): jnp.where(lax.axis_index(axis) == source, value, 0).astype(value.dtype)  7.95 us
    dot_general x4, matrix products, absorb(): jnp.einsum('hqk,kd->hqd', weights.astype(jnp.bfloat16), value_block, pref...  6.97 us
  transfers between devices with their start and end apart: 1, of which 1 were waited for; matrix products, arithmetic and copies ran while one was open for 0% of the time, Pallas kernels for 0%

commit v1 on v0

v1 whole, which is shorter than its diff:
```python
from functools import partial
import math

import jax
import jax.numpy as jnp
from jax import lax
from jax.experimental import pallas as pl
from jax.experimental.pallas import tpu as pltpu
from jax.sharding import PartitionSpec as P

HEAD_SIZE = 128
QUERY_PER_GROUP = 8
ADAPTER_RANK = 64
USED = 2

rope_base = 1000000.0

MESH = pl.DeviceIdType.MESH
BLOCK = 1024
LANE_ROWS = 16
SKEW = 2
OWN_CHUNKS = 35
ALL_CHUNKS = 53
QUARTER = 80


def chip_grid(chips):
    columns = 1
    while 2 * (2 * columns) ** 2 <= chips:
        columns *= 2
    return columns, chips // columns


def path_position(path, x, z, core, columns, rows):
    if path == 0:
        z = z + core * (rows - 1 - 2 * z)
        return x * rows + z + (x % 2) * (rows - 1 - 2 * z)
    x = x + core * (columns - 1 - 2 * x)
    return z * columns + x + (z % 2) * (columns - 1 - 2 * x)


def path_device(path, position, core, columns, rows):
    if path == 0:
        x = position // rows
        z = position % rows
        z = z + (x % 2) * (rows - 1 - 2 * z)
        z = z + core * (rows - 1 - 2 * z)
    else:
        z = position // columns
        x = position % columns
        x = x + (z % 2) * (columns - 1 - 2 * x)
        x = x + core * (columns - 1 - 2 * x)
    return (z * columns + x) * 2 + core


def chunk_place(k, quarter, grp):
    shared = k // OWN_CHUNKS
    kk = k - OWN_CHUNKS * shared
    group = kk // 8
    block = kk % 8
    narrow = shared * (group // 2)
    row = (
        QUARTER * quarter
        + LANE_ROWS * group
        + shared * (1 - group // 2) * (32 * grp)
        + narrow * 32
    )
    column = BLOCK * (block + narrow * 2 * grp)
    return shared, pl.multiple_of(row, LANE_ROWS), pl.multiple_of(column, BLOCK)


def fetch_kernel(
    seq_size,
    slots,
    ids_ref,
    holder_ref,
    entry_ref,
    x_ref,
    down_ref,
    up_ref,
    out_down_ref,
    out_up_ref,
    shrunk_ref,
    narrow_ref,
    wide_ref,
    own,
    mate_rows,
    moving,
    whole,
    load_sem,
    mate_send,
    mate_recv,
    chain_send,
    chain_recv,
    post_send,
    post_recv,
    cross_send,
    cross_recv,
):
    chips = seq_size // 2
    columns, rows = chip_grid(chips)
    grp = lax.axis_index("grp")
    me = lax.axis_index("seq")
    core = me % 2
    chip = me // 2
    x = chip % columns
    z = chip // columns
    mate = me + 1 - 2 * core
    other = 1 - grp
    positions = [path_position(j, x, z, core, columns, rows) for j in range(2)]

    def device_at(j, position):
        clipped = jnp.clip(position, 0, chips - 1)
        return path_device(j, clipped, core, columns, rows)

    following = [device_at(j, positions[j] + 1) for j in range(2)]
    preceding = [device_at(j, positions[j] - 1) for j in range(2)]

    loads = []
    for q in range(4):
        wide = down_ref.at[0, pl.ds(64 * q, 64)] if q < 3 else out_up_ref.at[0]
        loads.append((wide, own.at[pl.ds(QUARTER * q, 64)]))
        loads.append(
            (
                up_ref.at[0, pl.ds(16 * q, 16)],
                own.at[pl.ds(QUARTER * q + 64, 16), pl.ds(0, 1280)],
            )
        )
        loads.append(
            (
                out_down_ref.at[0, pl.ds(16 * q, 16)],
                own.at[pl.ds(QUARTER * q + 64, 16), pl.ds(1280, 1024)],
            )
        )
    loads = [
        pltpu.make_async_copy(source, target, load_sem.at[i])
        for i, (source, target) in enumerate(loads)
    ]
    for load in loads:
        load.start()
    for q in range(4):
        own[pl.ds(QUARTER * q + 64, 16), pl.ds(2304, 1792)] = jnp.zeros((16, 1792), jnp.bfloat16)

    barrier = pltpu.get_barrier_semaphore()

    def greet(device):
        pl.semaphore_signal(barrier, inc=1, device_id=device, device_id_type=MESH)

    greet((grp, mate))
    greet((other, me))
    greet((other, mate))
    expected = 3
    for j in range(2):

        @pl.when(positions[j] > 0)
        def _():
            greet((grp, preceding[j]))

        @pl.when(positions[j] < chips - 1)
        def _():
            greet((grp, following[j]))

        expected = expected + jnp.minimum(positions[j], 1)
        expected = expected + jnp.minimum(chips - 1 - positions[j], 1)

    rest = jnp.clip(ids_ref[0] + ids_ref[1] - (slots - 1), 0, slots - 1)
    owners = [holder_ref[rest], holder_ref[slots - 1]]
    mine = [jnp.where(owner == me, 1, 0) for owner in owners]
    mates = [jnp.where(owner == mate, 1, 0) for owner in owners]
    ahead = []
    for j in range(2):
        per_path = []
        for owner in owners:
            owner_chip = owner // 2
            place = path_position(
                j, owner_chip % columns, owner_chip // columns, core, columns, rows
            )
            per_path.append(jnp.where(place <= positions[j], 1, 0))
        ahead.append(per_path)
    picked = ids_ref[entry_ref[0]] == slots - 1

    pl.semaphore_wait(barrier, expected)
    for load in loads:
        load.wait()

    def mate_copy(j, group):
        source = 2 * (1 - core) + j
        return pltpu.make_async_remote_copy(
            src_ref=own.at[pl.ds(pl.multiple_of(QUARTER * source + 16 * group, 16), 16)],
            dst_ref=mate_rows.at[pl.ds(pl.multiple_of(QUARTER * j + 16 * group, 16), 16)],
            send_sem=mate_send,
            recv_sem=mate_recv.at[j * 5 + group],
            device_id=(grp, mate),
            device_id_type=MESH,
        )

    for group in range(5):
        for j in range(2):
            mate_copy(j, group).start()

    def chunk(d, j, k):
        return moving.at[d, j, pl.ds(pl.multiple_of(LANE_ROWS * k, LANE_ROWS), LANE_ROWS)]

    def chain_copy(d, j, k):
        return pltpu.make_async_remote_copy(
            src_ref=chunk(d, j, k),
            dst_ref=chunk(d, j, k),
            send_sem=chain_send.at[2 * d + j],
            recv_sem=chain_recv.at[(2 * d + j) * ALL_CHUNKS + k],
            device_id=(grp, following[j] if d == 0 else preceding[j]),
            device_id_type=MESH,
        )

    def post_copy(target, row, column, send_sem, recv_sem):
        piece = whole.at[pl.ds(row, LANE_ROWS), pl.ds(column, BLOCK)]
        return pltpu.make_async_remote_copy(
            src_ref=piece,
            dst_ref=piece,
            send_sem=send_sem,
            recv_sem=recv_sem,
            device_id=target,
            device_id_type=MESH,
        )

    def step(t, carry):
        @pl.when(jnp.logical_and(t % 8 == 0, t < 40))
        def _():
            for j in range(2):
                piece = mate_rows.at[pl.ds(0, 16)]
                pltpu.make_async_copy(piece, piece, mate_recv.at[j * 5 + t // 8]).wait()

        for j in range(2):
            for d in range(2):
                hops = positions[j] if d == 0 else chips - 1 - positions[j]
                k = t - SKEW * hops

                @pl.when(jnp.logical_and(k >= 0, k < ALL_CHUNKS))
                def _():
                    @pl.when(hops > 0)
                    def _():
                        chain_copy(d, j, k).wait_recv()

                    shared, row, column = chunk_place(k, 2 * core + j, grp)
                    mine_now = mine[0] + shared * (mine[1] - mine[0])
                    mate_now = mates[0] + shared * (mates[1] - mates[0])
                    here = own[pl.ds(row, LANE_ROWS), pl.ds(column, BLOCK)]
                    mate_row = pl.multiple_of(row - 2 * QUARTER * core, LANE_ROWS)
                    there = mate_rows[pl.ds(mate_row, LANE_ROWS), pl.ds(column, BLOCK)]
                    slot = pl.ds(pl.multiple_of(LANE_ROWS * k, LANE_ROWS), LANE_ROWS)
                    passed = moving[d, j, slot]
                    passed = lax.select_n(mate_now == 1, passed, there)
                    moving[d, j, slot] = lax.select_n(mine_now == 1, passed, here)

                    @pl.when(hops < chips - 1)
                    def _():
                        chain_copy(d, j, k).start()

            late = jnp.maximum(positions[j], chips - 1 - positions[j])
            done = t - SKEW * late

            @pl.when(jnp.logical_and(done >= 0, done < ALL_CHUNKS))
            def _():
                shared, row, column = chunk_place(done, 2 * core + j, grp)
                row = pl.multiple_of(row + 4 * QUARTER * shared, LANE_ROWS)
                slot = pl.ds(pl.multiple_of(LANE_ROWS * done, LANE_ROWS), LANE_ROWS)
                ahead_now = ahead[j][0] + shared * (ahead[j][1] - ahead[j][0])
                whole[pl.ds(row, LANE_ROWS), pl.ds(column, BLOCK)] = lax.select_n(
                    ahead_now == 1, moving[1, j, slot], moving[0, j, slot]
                )
                post_copy((grp, mate), row, column, post_send, post_recv).start()

                @pl.when(done >= OWN_CHUNKS)
                def _():
                    post_copy(
                        (other, me), row, column, cross_send.at[0], cross_recv.at[0]
                    ).start()
                    post_copy(
                        (other, mate), row, column, cross_send.at[1], cross_recv.at[1]
                    ).start()

        return carry

    lax.fori_loop(0, ALL_CHUNKS + SKEW * (chips - 1), step, 0)

    def drain(ref, sem):
        pltpu.make_async_copy(ref, ref, sem).wait()

    both = moving.at[0]
    cross = moving.at[0, :, pl.ds(0, LANE_ROWS * (ALL_CHUNKS - OWN_CHUNKS))]
    drain(both, post_recv)
    for i in range(2):
        drain(cross, cross_recv.at[i])

    total = jnp.zeros((x_ref.shape[0], 3 * ADAPTER_RANK), jnp.float32)

    def shrink(block, total):
        at = pl.ds(pl.multiple_of(block * BLOCK, BLOCK), BLOCK)
        parts = [
            lax.select_n(
                picked,
                whole[pl.ds(QUARTER * q, 64), at],
                whole[pl.ds(QUARTER * (4 + q), 64), at],
            )
            for q in range(3)
        ]
        return total + lax.dot_general(
            x_ref[:, at],
            jnp.concatenate(parts, 0),
            (((1,), (1,)), ((), ())),
            preferred_element_type=jnp.float32,
        )

    total = lax.fori_loop(0, x_ref.shape[1] // BLOCK, shrink, total)
    shrunk_ref[...] = total.astype(jnp.bfloat16)
    for q in range(4):
        at = pl.ds(0, 2304)
        narrow_ref[pl.ds(16 * q, 16), :] = lax.select_n(
            picked,
            whole[pl.ds(QUARTER * q + 64, 16), at],
            whole[pl.ds(QUARTER * (4 + q) + 64, 16), at],
        )

    def copy_wide(block, carry):
        at = pl.ds(pl.multiple_of(block * BLOCK, BLOCK), BLOCK)
        wide_ref[:, at] = lax.select_n(
            picked,
            whole[pl.ds(QUARTER * 3, 64), at],
            whole[pl.ds(QUARTER * 7, 64), at],
        )
        return carry

    lax.fori_loop(0, wide_ref.shape[1] // BLOCK, copy_wide, 0)

    drain(mate_rows, mate_send)
    for j in range(2):
        for d in range(2):
            hops = positions[j] if d == 0 else chips - 1 - positions[j]

            @pl.when(hops < chips - 1)
            def _():
                drain(moving.at[d, j], chain_send.at[2 * d + j])

    drain(both, post_send)
    for i in range(2):
        drain(cross, cross_send.at[i])


def rope_tables(positions, head_width):
    half_width = head_width // 2
    frequency = jnp.exp(
        jnp.arange(half_width, dtype=jnp.float32) * (-2.0 * math.log(rope_base) / head_width)
    )
    angles = positions.astype(jnp.float32)[:, None] * frequency[None, :]
    return (jnp.cos(angles), jnp.sin(angles))


def rotate(vectors, cosine, sine_table):
    half_width = vectors.shape[-1] // 2
    first_half = vectors[..., :half_width]
    second_half = vectors[..., half_width:]
    return jnp.concatenate(
        [
            first_half * cosine - second_half * sine_table,
            second_half * cosine + first_half * sine_table,
        ],
        -1,
    )


def absorb(states, queries, positions, key_block, value_block, key_start):
    maxima, totals, summed = states
    scores = jnp.einsum(
        "qhd,kd->hqk", queries, key_block, preferred_element_type=jnp.float32
    ) * HEAD_SIZE ** (-0.5)
    visible = (key_start + jnp.arange(key_block.shape[0], dtype=jnp.int32))[None, :] <= positions[
        :, None
    ]
    scores = jnp.where(visible[None], scores, -1e30)
    new_maxima = jnp.maximum(maxima, jnp.max(scores, -1))
    weights = jnp.where(visible[None], jnp.exp(scores - new_maxima[:, :, None]), 0.0)
    rescale = jnp.exp(maxima - new_maxima)
    totals = totals * rescale + jnp.sum(weights, -1)
    summed = summed * rescale[:, :, None] + jnp.einsum(
        "hqk,kd->hqd", weights.astype(jnp.bfloat16), value_block, preferred_element_type=jnp.float32
    )
    return (new_maxima, totals, summed)


def shards(
    seq_size,
    normed_input,
    base_projection_weight,
    adapter_down_pool,
    adapter_up_pool,
    output_down_pool,
    output_up_pool,
    request_adapter_ids,
    holder,
    segment_adapter_entry,
):
    tok_rows, width = normed_input.shape
    query_width = QUERY_PER_GROUP * HEAD_SIZE
    slots = holder.shape[0]
    in_smem = pl.BlockSpec(memory_space=pltpu.SMEM)
    in_vmem = pl.BlockSpec(memory_space=pltpu.VMEM)
    in_any = pl.BlockSpec(memory_space=pl.ANY)
    bf16 = jnp.bfloat16
    reduced_rank_rows, narrow, out_up = pl.pallas_call(
        partial(fetch_kernel, seq_size, slots),
        out_shape=(
            jax.ShapeDtypeStruct((tok_rows, 3 * ADAPTER_RANK), bf16),
            jax.ShapeDtypeStruct((ADAPTER_RANK, 2304), bf16),
            jax.ShapeDtypeStruct((ADAPTER_RANK, width), bf16),
        ),
        in_specs=[in_smem] * 3 + [in_vmem] + [in_any] * 4,
        out_specs=(in_vmem, in_vmem, in_vmem),
        scratch_shapes=[
            pltpu.VMEM((4 * QUARTER, width), bf16),
            pltpu.VMEM((2 * QUARTER, width), bf16),
            pltpu.VMEM((2, 2, LANE_ROWS * ALL_CHUNKS, BLOCK), bf16),
            pltpu.VMEM((8 * QUARTER, width), bf16),
            pltpu.SemaphoreType.DMA((12,)),
            pltpu.SemaphoreType.DMA,
            pltpu.SemaphoreType.DMA((10,)),
            pltpu.SemaphoreType.DMA((4,)),
            pltpu.SemaphoreType.DMA((4 * ALL_CHUNKS,)),
            pltpu.SemaphoreType.DMA,
            pltpu.SemaphoreType.DMA,
            pltpu.SemaphoreType.DMA((2,)),
            pltpu.SemaphoreType.DMA((2,)),
        ],
        compiler_params=pltpu.CompilerParams(
            collective_id=0, has_side_effects=True, vmem_limit_bytes=48 * 1024 * 1024
        ),
        name="fetch",
    )(
        request_adapter_ids,
        holder,
        segment_adapter_entry,
        normed_input,
        adapter_down_pool,
        adapter_up_pool,
        output_down_pool,
        output_up_pool,
    )
    up_weight = narrow[:, : query_width + 2 * HEAD_SIZE]
    out_down = narrow[:, query_width + 2 * HEAD_SIZE :]
    delta_query = jnp.dot(
        reduced_rank_rows[:, :ADAPTER_RANK],
        up_weight[:, :query_width],
        preferred_element_type=jnp.float32,
    )
    delta_key = jnp.dot(
        reduced_rank_rows[:, ADAPTER_RANK : 2 * ADAPTER_RANK],
        up_weight[:, query_width : query_width + HEAD_SIZE],
        preferred_element_type=jnp.float32,
    )
    delta_value = jnp.dot(
        reduced_rank_rows[:, 2 * ADAPTER_RANK :],
        up_weight[:, query_width + HEAD_SIZE :],
        preferred_element_type=jnp.float32,
    )
    deltas = jnp.concatenate([delta_query, delta_key, delta_value], 1)
    combined = base_projection_weight.astype(jnp.float32) + deltas
    device_index = lax.axis_index("seq")
    positions = device_index * tok_rows + jnp.arange(tok_rows, dtype=jnp.int32)
    cosine, sine_table = rope_tables(positions, HEAD_SIZE)
    queries = rotate(
        combined[:, :query_width].reshape(tok_rows, QUERY_PER_GROUP, HEAD_SIZE),
        cosine[:, None, :],
        sine_table[:, None, :],
    ).astype(jnp.bfloat16)
    key_rows = rotate(
        combined[:, query_width : query_width + HEAD_SIZE], cosine, sine_table
    ).astype(jnp.bfloat16)
    value_rows = combined[:, query_width + HEAD_SIZE :].astype(jnp.bfloat16)
    initial = (
        jnp.full((QUERY_PER_GROUP, tok_rows), -1e30, jnp.float32),
        jnp.zeros((QUERY_PER_GROUP, tok_rows), jnp.float32),
        jnp.zeros((QUERY_PER_GROUP, tok_rows, HEAD_SIZE), jnp.float32),
    )
    pair = lax.all_gather(
        jnp.concatenate([key_rows, value_rows], 1), "seq", axis=0, tiled=True
    )
    piece_rows = pair.shape[0]
    block_rows = math.gcd(piece_rows, 512)

    def one_block(block_index, states):
        local_start = block_index * block_rows
        block = lax.dynamic_slice_in_dim(pair, local_start, block_rows, 0)
        return lax.cond(
            local_start <= positions[-1],
            partial(
                absorb,
                queries=queries,
                positions=positions,
                key_block=block[:, :HEAD_SIZE],
                value_block=block[:, HEAD_SIZE:],
                key_start=local_start,
            ),
            lambda states: states,
            states,
        )

    maxima, totals, summed = lax.fori_loop(0, piece_rows // block_rows, one_block, initial)
    normalized = (summed / totals[:, :, None]).transpose(1, 0, 2)
    attended = normalized.reshape(tok_rows, query_width).astype(jnp.bfloat16)
    reduced_out_rows = lax.dot_general(
        attended, out_down, (((1,), (1,)), ((), ())), preferred_element_type=jnp.float32
    ).astype(jnp.bfloat16)
    out_rows = jnp.dot(reduced_out_rows, out_up, preferred_element_type=jnp.float32).astype(
        jnp.bfloat16
    )
    return (attended, out_rows)


def solution(mesh):
    in_specs = (
        P(("grp", "seq"), None),
        P(("grp", "seq"), None),
        P("seq", None, None),
        P("seq", None, None),
        P("seq", None, None),
        P("seq", None, None),
        P("grp"),
        P(),
        P(("grp", "seq")),
    )
    out_specs = (P(("grp", "seq"), None), P(("grp", "seq"), None))
    return jax.shard_map(
        partial(shards, mesh.shape["seq"]),
        mesh=mesh,
        in_specs=in_specs,
        out_specs=out_specs,
        check_vma=False,
    )
```

time: 280 us -> 204 us (0.73)
  waiting for transfers between devices: 181 us -> 36.1 us
  Pallas kernels: 0 us -> 120 us
  blocking collectives: 41 us -> 0 us
  other arithmetic: 12.6 us -> 4.34 us
  between operations: 20.1 us -> 14.8 us
  local copies, waits for them, and re-layouts: 5.49 us -> 8.81 us
    psum x1 -> x0, waiting for transfers between devices: 181 us -> none  [spread(): return lax.psum(kept, axis)]
    pallas_call x0 -> x1, Pallas kernels: none -> 120 us  [shards(): pl.pallas_call(partial(fetch_kernel, seq_size, slots), out_shape=(jax.Sha...]
    all_gather x2 -> x0, blocking collectives: 41 us -> none  [the longest x1 23.1 us: shards(): value_piece = lax.all_gather(value_rows, 'seq', axis=0, tiled=True)]
    all_gather x0 -> x1, waiting for transfers between devices: none -> 36.1 us  [shards(): lax.all_gather(jnp.concatenate([key_rows, value_rows], 1), 'seq', axis=0,...]
    select_n x4 -> x0, other arithmetic: 7.95 us -> none  [spread(): jnp.where(lax.axis_index(axis) == source, value, 0).astype(value.dtype)]
    unnamed x16 -> x18, local copies, waits for them, and re-layouts: 0.18 us -> 6.09 us
    dot_general x2 -> x1, matrix products: 7.03 us -> 2.31 us  [shards(): jnp.dot(reduced_out_rows, out_up, preferred_element_type=jnp.float32)]
    dot_general x4, matrix products: 1.82 us -> 5.45 us  [absorb(): jnp.einsum('qhd,kd->hqk', queries, key_block, preferred_element_type=jnp....]
where the time goes in v1:
time: 204 us; the launch traced here: 203 us
  Pallas kernels  120 us (59%)
  waiting for transfers between devices  36.1 us (18%)
  matrix products  15.3 us (8%)
  between operations  14.8 us (7%)
  local copies, waits for them, and re-layouts  8.81 us (4%)
  other arithmetic  4.34 us (2%)
  loops' own time  2.96 us (1%)
    pallas_call x1, Pallas kernels, shards(): pl.pallas_call(partial(fetch_kernel, seq_size, slots), out_shape=(jax.Sha...  120 us
    all_gather x1, waiting for transfers between devices, shards(): lax.all_gather(jnp.concatenate([key_rows, value_rows], 1), 'seq', axis=0,...  36.1 us
    dot_general x4, matrix products, absorb(): jnp.einsum('hqk,kd->hqd', weights.astype(jnp.bfloat16), value_block, pref...  6.98 us
    unnamed x18, local copies, waits for them, and re-layouts  6.09 us
    dot_general x4, matrix products, absorb(): jnp.einsum('qhd,kd->hqk', queries, key_block, preferred_element_type=jnp....  5.45 us
  transfers between devices with their start and end apart: 1, of which 1 were waited for; matrix products, arithmetic and copies ran while one was open for 0% of the time, Pallas kernels for 0%

profile of v1, /device:TPU:27, one launch (start us, length us, event | category | flops | bytes accessed | tf_op | source)
XLA Modules:
  0.0 202.7 jit_solution(14259425809530455130)
XLA Ops:
  7.2 0.0 all-gather.2.cloned.1.call-start
  7.9 1.6 copy-done
  9.5 1.2 copy-done.1
  10.7 0.9 copy-done.2
  11.6 0.9 copy-done.3
  12.5 0.7 copy-done.4
  13.2 0.7 copy-done.5
  13.8 120.4 %fetch.1 = (bf16[128,192]{1,0:T(8,128)(2,1)S(1)}, bf16[64,2304]{1,0:T(8,128)(2,1)S(1)}, bf16[64,8192]{1,0:T(8,128)(2,1)S(1)}) custom-call(s32[2]{0:T(128)S(1)} %copy-done.4, s32[16]{0:T(128)S(1)} %copy-done.5, s32[1]{0:T(128)S(6)} %copy.48.entry_ref, bf16[128,8192]{1,0:T(8,128)(2,1)S(1)} %copy-done, bf16[1,192,8192]{2,1,0:T(8,128)(2,1)} %down_ref.1, ...), custom_call_target="tpu_custom_call" | custom-call | tf_op jit(solution)/shard_map/fetch/pallas_call | solution.py:408
  134.2 0.1 fusion.18
  134.3 0.2 fusion.20
  134.5 0.2 fusion.16
  134.8 0.1 maximum_add_fusion
  134.9 0.3 multiply_cosine_fusion
  135.2 0.7 pad_maximum_fusion.1
  135.9 0.0 all-gather.2.cloned.1.call-update
  136.0 0.1 copy.23
  136.1 0.2 fusion.26
  136.3 0.2 subtract_convert_fusion
  136.5 0.1 pad_maximum_fusion
  136.7 36.1 %all-gather.2.cloned.1.call-done = bf16[2048,256]{1,0:T(8,128)(2,1)} async-done(((bf16[128,256]{1,0:T(8,128)(2,1)}), bf16[2048,256]{1,0:T(8,128)(2,1)}) %all-gather.2.cloned.1.call-update) | async-done | bytes 1048592 | tf_op jit(solution)/shard_map/all_gather | solution.py:482
  172.8 20.5 %while.17 = (s32[]{:T(128)}, f32[8,128]{1,0:T(8,128)S(1)}, f32[8,128]{1,0:T(8,128)S(1)}, f32[8,128,128]{2,1,0:T(8,128)S(1)}, s32[128]{0:T(128)S(1)}, /*index=5*/...) while((s32[]{:T(128)}, f32[8,128]{1,0:T(8,128)S(1)}, ...), condition=%wide.region_5.6_spmd, body=%wide.region_0.5_spmd.sunk | while | flops 275581440 | bytes 8196909 | solution.py:505
  172.8 0.6 slice.118
  174.1 3.9 %conditional.2 = ((f32[8,128]{1,0:T(8,128)S(1)}, f32[8,128]{1,0:T(8,128)S(1)}, f32[8,128,128]{2,1,0:T(8,128)S(1)})) conditional(s32[]{:T(128)} %convert_element_type.60, (f32[8,128]{1,0:T(8,128)S(1)}, f32[8,128]{1,0:T(8,128)S(1)}, f32[8,128,128]{2,1,0:T(8,128)S(1)}) %tuple.55, (s32[]{:T(128)}, s32[128]{0:T(128)S(1)}, bf16[2048,256]{1,0:T(8,128)(2,1)}, ...), branch_computations={%region_1.0_spmd, %region_2.4_spmd} | conditional | flops 275581440 | bytes 8196702 | solution.py:491
  174.1 0.1 broadcast_compare_fusion
  174.3 1.4 fusion
  175.6 0.5 fusion.2
  176.2 1.7 convolution_add_fusion
  178.0 0.6 slice.118
  179.2 3.9 %conditional.2 = ((f32[8,128]{1,0:T(8,128)S(1)}, f32[8,128]{1,0:T(8,128)S(1)}, f32[8,128,128]{2,1,0:T(8,128)S(1)})) conditional(s32[]{:T(128)} %convert_element_type.60, (f32[8,128]{1,0:T(8,128)S(1)}, f32[8,128]{1,0:T(8,128)S(1)}, f32[8,128,128]{2,1,0:T(8,128)S(1)}) %tuple.55, (s32[]{:T(128)}, s32[128]{0:T(128)S(1)}, bf16[2048,256]{1,0:T(8,128)(2,1)}, ...), branch_computations={%region_1.0_spmd, %region_2.4_spmd} | conditional | flops 275581440 | bytes 8196702 | solution.py:491
  179.2 0.1 broadcast_compare_fusion
  179.4 1.4 fusion
  180.8 0.5 fusion.2
  181.3 1.7 convolution_add_fusion
  183.1 0.6 slice.118
  184.3 3.9 %conditional.2 = ((f32[8,128]{1,0:T(8,128)S(1)}, f32[8,128]{1,0:T(8,128)S(1)}, f32[8,128,128]{2,1,0:T(8,128)S(1)})) conditional(s32[]{:T(128)} %convert_element_type.60, (f32[8,128]{1,0:T(8,128)S(1)}, f32[8,128]{1,0:T(8,128)S(1)}, f32[8,128,128]{2,1,0:T(8,128)S(1)}) %tuple.55, (s32[]{:T(128)}, s32[128]{0:T(128)S(1)}, bf16[2048,256]{1,0:T(8,128)(2,1)}, ...), branch_computations={%region_1.0_spmd, %region_2.4_spmd} | conditional | flops 275581440 | bytes 8196702 | solution.py:491
  184.4 0.1 broadcast_compare_fusion
  184.5 1.4 fusion
  185.9 0.5 fusion.2
  186.4 1.7 convolution_add_fusion
  188.2 0.6 slice.118
  189.5 3.9 %conditional.2 = ((f32[8,128]{1,0:T(8,128)S(1)}, f32[8,128]{1,0:T(8,128)S(1)}, f32[8,128,128]{2,1,0:T(8,128)S(1)})) conditional(s32[]{:T(128)} %convert_element_type.60, (f32[8,128]{1,0:T(8,128)S(1)}, f32[8,128]{1,0:T(8,128)S(1)}, f32[8,128,128]{2,1,0:T(8,128)S(1)}) %tuple.55, (s32[]{:T(128)}, s32[128]{0:T(128)S(1)}, bf16[2048,256]{1,0:T(8,128)(2,1)}, ...), branch_computations={%region_1.0_spmd, %region_2.4_spmd} | conditional | flops 275581440 | bytes 8196702 | solution.py:491
  189.5 0.1 broadcast_compare_fusion
  189.6 1.4 fusion
  191.0 0.5 fusion.2
  191.6 1.7 convolution_add_fusion
  193.3 0.2 copy_bitcast_fusion
  193.5 0.0 copy-start.6
  193.6 2.3 %convolution_convert_fusion = bf16[128,8192]{1,0:T(8,128)(2,1)} fusion(bf16[64,8192]{1,0:T(8,128)(2,1)S(1)} %get-tuple-element.223, bf16[128,1024]{1,0:T(8,128)(2,1)S(1)} %copy_bitcast_fusion, bf16[64,2304]{1,0:T(8,128)(2,1)S(1)} %get-tuple-element.220), kind=kOutput, calls=%fused_computation.21 | convolution fusion | flops 152051712 | bytes 3538944 | tf_op jit(solution)/shard_map/dot_general | solution.py:511
  (33 shorter events, 0.2 us)
Async XLA Ops:
  7.2 165.6 %all-gather.2.cloned.1.call-start = ((), (), s32[]{:S(2)}) async-start(), calls=%async_computation | async-start | bytes 1114112 | tf_op jit(solution)/shard_map/all_gather | solution.py:482
  7.9 1.6 copy-start
  9.5 1.2 copy-start.1
  10.7 0.9 copy-start.2
  11.6 0.9 copy-start.3
  12.5 0.7 copy-start.4
  13.2 0.7 copy-start.5
  13.8 120.9 %copy-start.7 = (bf16[128,1280]{1,0:T(8,128)(2,1)S(1)}, bf16[128,1280]{1,0:T(8,128)(2,1)}, u32[]{:S(2)}) copy-start(bf16[128,1280]{1,0:T(8,128)(2,1)} %param.14) | copy-start | bytes 983044
  193.5 2.3 %copy-start.6 = (bf16[128,1024]{1,0:T(8,128)(2,1)}, bf16[128,1024]{1,0:T(8,128)(2,1)S(1)}, u32[]{:S(2)}) copy-start(bf16[128,1024]{1,0:T(8,128)(2,1)S(1)} %copy_bitcast_fusion) | copy-start | bytes 786436
Sparse Core Ops, SparseCore 0:
  136.0 36.6 all-gather.1

commit v2 on v1

--- a/solution.py
+++ b/solution.py
@@ -16,11 +16,11 @@
 rope_base = 1000000.0
 
 MESH = pl.DeviceIdType.MESH
-BLOCK = 1024
+BLOCK = 2048
 LANE_ROWS = 16
 SKEW = 2
-OWN_CHUNKS = 35
-ALL_CHUNKS = 53
+SHARED_CHUNKS = 9
+ALL_CHUNKS = 27
 QUARTER = 80
 
 
@@ -54,10 +54,10 @@
 
 
 def chunk_place(k, quarter, grp):
-    shared = k // OWN_CHUNKS
-    kk = k - OWN_CHUNKS * shared
-    group = kk // 8
-    block = kk % 8
+    shared = 1 - jnp.minimum(k // SHARED_CHUNKS, 1)
+    kk = k - SHARED_CHUNKS * (1 - shared)
+    group = kk // 4
+    block = kk % 4
     narrow = shared * (group // 2)
     row = (
         QUARTER * quarter
@@ -65,7 +65,7 @@
         + shared * (1 - group // 2) * (32 * grp)
         + narrow * 32
     )
-    column = BLOCK * (block + narrow * 2 * grp)
+    column = BLOCK * (block + narrow * grp)
     return shared, pl.multiple_of(row, LANE_ROWS), pl.multiple_of(column, BLOCK)
 
 
@@ -183,20 +183,21 @@
     for load in loads:
         load.wait()
 
-    def mate_copy(j, group):
+    def mate_copy(j, order):
+        group = [2 * grp, 2 * grp + 1, 4, 2 - 2 * grp, 3 - 2 * grp][order]
         source = 2 * (1 - core) + j
         return pltpu.make_async_remote_copy(
             src_ref=own.at[pl.ds(pl.multiple_of(QUARTER * source + 16 * group, 16), 16)],
             dst_ref=mate_rows.at[pl.ds(pl.multiple_of(QUARTER * j + 16 * group, 16), 16)],
             send_sem=mate_send,
-            recv_sem=mate_recv.at[j * 5 + group],
+            recv_sem=mate_recv.at[j * 5 + order],
             device_id=(grp, mate),
             device_id_type=MESH,
         )
 
-    for group in range(5):
+    for order in range(5):
         for j in range(2):
-            mate_copy(j, group).start()
+            mate_copy(j, order).start()
 
     def chunk(d, j, k):
         return moving.at[d, j, pl.ds(pl.multiple_of(LANE_ROWS * k, LANE_ROWS), LANE_ROWS)]
@@ -223,11 +224,13 @@
         )
 
     def step(t, carry):
-        @pl.when(jnp.logical_and(t % 8 == 0, t < 40))
-        def _():
-            for j in range(2):
-                piece = mate_rows.at[pl.ds(0, 16)]
-                pltpu.make_async_copy(piece, piece, mate_recv.at[j * 5 + t // 8]).wait()
+        for at_step, orders in ((0, (0,)), (4, (1,)), (8, (2, 3, 4))):
+
+            @pl.when(t == at_step)
+            def _():
+                for order in orders:
+                    for j in range(2):
+                        mate_copy(j, order).wait_recv()
 
         for j in range(2):
             for d in range(2):
@@ -269,7 +272,7 @@
                 )
                 post_copy((grp, mate), row, column, post_send, post_recv).start()
 
-                @pl.when(done >= OWN_CHUNKS)
+                @pl.when(done < SHARED_CHUNKS)
                 def _():
                     post_copy(
                         (other, me), row, column, cross_send.at[0], cross_recv.at[0]
@@ -286,7 +289,7 @@
         pltpu.make_async_copy(ref, ref, sem).wait()
 
     both = moving.at[0]
-    cross = moving.at[0, :, pl.ds(0, LANE_ROWS * (ALL_CHUNKS - OWN_CHUNKS))]
+    cross = moving.at[0, :, pl.ds(0, LANE_ROWS * SHARED_CHUNKS)]
     drain(both, post_recv)
     for i in range(2):
         drain(cross, cross_recv.at[i])
@@ -354,36 +357,195 @@
     return (jnp.cos(angles), jnp.sin(angles))
 
 
-def rotate(vectors, cosine, sine_table):
-    half_width = vectors.shape[-1] // 2
-    first_half = vectors[..., :half_width]
-    second_half = vectors[..., half_width:]
-    return jnp.concatenate(
-        [
-            first_half * cosine - second_half * sine_table,
-            second_half * cosine + first_half * sine_table,
-        ],
-        -1,
-    )
-
-
-def absorb(states, queries, positions, key_block, value_block, key_start):
-    maxima, totals, summed = states
-    scores = jnp.einsum(
-        "qhd,kd->hqk", queries, key_block, preferred_element_type=jnp.float32
-    ) * HEAD_SIZE ** (-0.5)
-    visible = (key_start + jnp.arange(key_block.shape[0], dtype=jnp.int32))[None, :] <= positions[
-        :, None
-    ]
-    scores = jnp.where(visible[None], scores, -1e30)
-    new_maxima = jnp.maximum(maxima, jnp.max(scores, -1))
-    weights = jnp.where(visible[None], jnp.exp(scores - new_maxima[:, :, None]), 0.0)
-    rescale = jnp.exp(maxima - new_maxima)
-    totals = totals * rescale + jnp.sum(weights, -1)
-    summed = summed * rescale[:, :, None] + jnp.einsum(
-        "hqk,kd->hqd", weights.astype(jnp.bfloat16), value_block, preferred_element_type=jnp.float32
-    )
-    return (new_maxima, totals, summed)
+def attend_kernel(
+    seq_size,
+    shrunk_ref,
+    narrow_ref,
+    base_ref,
+    cosine_ref,
+    sine_ref,
+    attended_ref,
+    out_shrunk_ref,
+    pairs,
+    queries,
+    maxima,
+    totals,
+    summed,
+    line_send,
+    cross_send,
+    mate_send,
+    recv,
+):
+    columns, rows = chip_grid(seq_size // 2)
+    grp = lax.axis_index("grp")
+    me = lax.axis_index("seq")
+    core = me % 2
+    x = (me // 2) % columns
+    z = me // (2 * columns)
+    mate = me + 1 - 2 * core
+    tokens = base_ref.shape[0]
+    query_width = QUERY_PER_GROUP * HEAD_SIZE
+    level = 2 * columns * tokens
+
+    def device(z, x, core):
+        return (z * columns + x) * 2 + core
+
+    barrier = pltpu.get_barrier_semaphore()
+
+    def greet(other):
+        pl.semaphore_signal(barrier, inc=1, device_id=(grp, other), device_id_type=MESH)
+
+    def greet_line(i, carry):
+        greet(device((z + i) % rows, x, core))
+        return carry
+
+    lax.fori_loop(1, rows, greet_line, 0)
+    for i in range(1, columns):
+        greet(device(z, (x + i) % columns, core))
+    greet(mate)
+
+    rank = ADAPTER_RANK
+
+    def project(first, width, member):
+        return base_ref[:, pl.ds(first, width)].astype(jnp.float32) + jnp.dot(
+            shrunk_ref[:, member * rank : (member + 1) * rank],
+            narrow_ref[:, pl.ds(first, width)],
+            preferred_element_type=jnp.float32,
+        )
+
+    cosine = cosine_ref[...]
+    sine = sine_ref[...]
+
+    def turn(vectors):
+        swapped = pltpu.roll(vectors, HEAD_SIZE // 2, 1)
+        return (vectors * cosine + swapped * sine).astype(jnp.bfloat16)
+
+    def rows_of(owner):
+        return pl.ds(pl.multiple_of(owner * tokens, tokens), tokens)
+
+    pairs[rows_of(me), pl.ds(0, HEAD_SIZE)] = turn(project(query_width, HEAD_SIZE, 1))
+    pairs[rows_of(me), pl.ds(HEAD_SIZE, HEAD_SIZE)] = project(
+        query_width + HEAD_SIZE, HEAD_SIZE, 2
+    ).astype(jnp.bfloat16)
+
+    pl.semaphore_wait(barrier, rows - 1 + columns - 1 + 1)
+
+    def send(owner, target, send_sem):
+        return pltpu.make_async_remote_copy(
+            src_ref=pairs.at[rows_of(owner)],
+            dst_ref=pairs.at[rows_of(owner)],
+            send_sem=send_sem,
+            recv_sem=recv.at[owner],
+            device_id=(grp, target),
+            device_id_type=MESH,
+        )
+
+    def to_line(later):
+        return send(me, device(later, x, core), line_send.at[later])
+
+    def to_row(deep, i):
+        return send(
+            device(deep, x, core),
+            device(z, (x + i) % columns, core),
+            cross_send.at[deep * columns + i],
+        )
+
+    def to_mate(deep, i):
+        i = (x + i) % columns
+        return send(device(deep, i, core), mate, mate_send.at[deep * columns + i])
+
+    def await_pair(owner):
+        piece = pairs.at[rows_of(owner)]
+        pltpu.make_async_copy(piece, piece, recv.at[owner]).wait()
+
+    def relay(deep):
+        for i in range(1, columns):
+            to_row(deep, i).start()
+        to_mate(deep, 0).start()
+
+    def start_line(later, carry):
+        to_line(later).start()
+        return carry
+
+    relay(z)
+    lax.fori_loop(z + 1, rows, start_line, 0)
+
+    for h in range(QUERY_PER_GROUP):
+        queries[pl.ds(h * tokens, tokens), :] = turn(project(h * HEAD_SIZE, HEAD_SIZE, 0))
+    maxima[...] = jnp.full_like(maxima, -1e30)
+    totals[...] = jnp.zeros_like(totals)
+    summed[...] = jnp.zeros_like(summed)
+
+    together = 2 * tokens
+
+    def one_level(o, carry):
+        deep = z - o
+
+        @pl.when(o < z)
+        def _():
+            await_pair(device(deep - 1, x, core))
+            relay(deep - 1)
+
+        for i in range(1, columns):
+            await_pair(device(deep, (x + i) % columns, core))
+            to_mate(deep, i).start()
+        for i in range(columns):
+            await_pair(device(deep, i, 1 - core))
+
+        at = pl.ds(pl.multiple_of(deep * level, level), level)
+        keys = pairs[at, pl.ds(0, HEAD_SIZE)]
+        values = pairs[at, pl.ds(HEAD_SIZE, HEAD_SIZE)]
+        key_place = deep * level + lax.broadcasted_iota(jnp.int32, (together, level), 1)
+        row_place = me * tokens + lax.broadcasted_iota(jnp.int32, (together, level), 0) % tokens
+        visible = key_place <= row_place
+        for first in range(0, QUERY_PER_GROUP * tokens, together):
+            here = pl.ds(first, together)
+            scores = lax.dot_general(
+                queries[here, :],
+                keys,
+                (((1,), (1,)), ((), ())),
+                preferred_element_type=jnp.float32,
+            ) * HEAD_SIZE ** (-0.5)
+            scores = jnp.where(visible, scores, -1e30)
+            before = maxima[here, :]
+            now = jnp.maximum(before, jnp.max(scores, 1, keepdims=True))
+            weights = jnp.where(visible, jnp.exp(scores - now), 0.0)
+            rescale = jnp.exp(before - now)
+            maxima[here, :] = now
+            totals[here, :] = totals[here, :] * rescale + jnp.sum(weights, 1, keepdims=True)
+            summed[here, :] = summed[here, :] * rescale + jnp.dot(
+                weights.astype(jnp.bfloat16), values, preferred_element_type=jnp.float32
+            )
+        return carry
+
+    lax.fori_loop(0, z + 1, one_level, 0)
+
+    for h in range(QUERY_PER_GROUP):
+        here = pl.ds(h * tokens, tokens)
+        attended_ref[:, pl.ds(h * HEAD_SIZE, HEAD_SIZE)] = (
+            summed[here, :] / totals[here, :]
+        ).astype(jnp.bfloat16)
+    out_shrunk_ref[...] = lax.dot_general(
+        attended_ref[...],
+        narrow_ref[:, pl.ds(query_width + 2 * HEAD_SIZE, query_width)],
+        (((1,), (1,)), ((), ())),
+        preferred_element_type=jnp.float32,
+    ).astype(jnp.bfloat16)
+
+    def end_line(later, carry):
+        to_line(later).wait_send()
+        return carry
+
+    lax.fori_loop(z + 1, rows, end_line, 0)
+
+    def end_level(deep, carry):
+        for i in range(1, columns):
+            to_row(deep, i).wait_send()
+        for i in range(columns):
+            to_mate(deep, i).wait_send()
+        return carry
+
+    lax.fori_loop(0, z + 1, end_level, 0)
 
 
 def shards(
@@ -430,7 +592,7 @@
             pltpu.SemaphoreType.DMA((2,)),
         ],
         compiler_params=pltpu.CompilerParams(
-            collective_id=0, has_side_effects=True, vmem_limit_bytes=48 * 1024 * 1024
+            collective_id=0, has_side_effects=True, vmem_limit_bytes=60 * 1024 * 1024
         ),
         name="fetch",
     )(
@@ -443,71 +605,40 @@
         output_down_pool,
         output_up_pool,
     )
-    up_weight = narrow[:, : query_width + 2 * HEAD_SIZE]
-    out_down = narrow[:, query_width + 2 * HEAD_SIZE :]
-    delta_query = jnp.dot(
-        reduced_rank_rows[:, :ADAPTER_RANK],
-        up_weight[:, :query_width],
-        preferred_element_type=jnp.float32,
+    positions = lax.axis_index("seq") * tok_rows + jnp.arange(tok_rows, dtype=jnp.int32)
+    cosine, sine = rope_tables(positions, HEAD_SIZE)
+    columns, rows = chip_grid(seq_size // 2)
+    heads = QUERY_PER_GROUP * tok_rows
+    attended, reduced_out_rows = pl.pallas_call(
+        partial(attend_kernel, seq_size),
+        out_shape=(
+            jax.ShapeDtypeStruct((tok_rows, query_width), bf16),
+            jax.ShapeDtypeStruct((tok_rows, ADAPTER_RANK), bf16),
+        ),
+        in_specs=[in_vmem] * 5,
+        out_specs=(in_vmem, in_vmem),
+        scratch_shapes=[
+            pltpu.VMEM((seq_size * tok_rows, 2 * HEAD_SIZE), bf16),
+            pltpu.VMEM((heads, HEAD_SIZE), bf16),
+            pltpu.VMEM((heads, 1), jnp.float32),
+            pltpu.VMEM((heads, 1), jnp.float32),
+            pltpu.VMEM((heads, HEAD_SIZE), jnp.float32),
+            pltpu.SemaphoreType.DMA((rows,)),
+            pltpu.SemaphoreType.DMA((rows * columns,)),
+            pltpu.SemaphoreType.DMA((rows * columns,)),
+            pltpu.SemaphoreType.DMA((seq_size,)),
+        ],
+        compiler_params=pltpu.CompilerParams(
+            collective_id=1, has_side_effects=True, vmem_limit_bytes=40 * 1024 * 1024
+        ),
+        name="attend",
+    )(
+        reduced_rank_rows,
+        narrow,
+        base_projection_weight,
+        jnp.concatenate([cosine, cosine], 1),
+        jnp.concatenate([-sine, sine], 1),
     )
-    delta_key = jnp.dot(
-        reduced_rank_rows[:, ADAPTER_RANK : 2 * ADAPTER_RANK],
-        up_weight[:, query_width : query_width + HEAD_SIZE],
-        preferred_element_type=jnp.float32,
-    )
-    delta_value = jnp.dot(
-        reduced_rank_rows[:, 2 * ADAPTER_RANK :],
-        up_weight[:, query_width + HEAD_SIZE :],
-        preferred_element_type=jnp.float32,
-    )
-    deltas = jnp.concatenate([delta_query, delta_key, delta_value], 1)
-    combined = base_projection_weight.astype(jnp.float32) + deltas
-    device_index = lax.axis_index("seq")
-    positions = device_index * tok_rows + jnp.arange(tok_rows, dtype=jnp.int32)
-    cosine, sine_table = rope_tables(positions, HEAD_SIZE)
-    queries = rotate(
-        combined[:, :query_width].reshape(tok_rows, QUERY_PER_GROUP, HEAD_SIZE),
-        cosine[:, None, :],
-        sine_table[:, None, :],
-    ).astype(jnp.bfloat16)
-    key_rows = rotate(
-        combined[:, query_width : query_width + HEAD_SIZE], cosine, sine_table
-    ).astype(jnp.bfloat16)
-    value_rows = combined[:, query_width + HEAD_SIZE :].astype(jnp.bfloat16)
-    initial = (
-        jnp.full((QUERY_PER_GROUP, tok_rows), -1e30, jnp.float32),
-        jnp.zeros((QUERY_PER_GROUP, tok_rows), jnp.float32),
-        jnp.zeros((QUERY_PER_GROUP, tok_rows, HEAD_SIZE), jnp.float32),
-    )
-    pair = lax.all_gather(
-        jnp.concatenate([key_rows, value_rows], 1), "seq", axis=0, tiled=True
-    )
-    piece_rows = pair.shape[0]
-    block_rows = math.gcd(piece_rows, 512)
-
-    def one_block(block_index, states):
-        local_start = block_index * block_rows
-        block = lax.dynamic_slice_in_dim(pair, local_start, block_rows, 0)
-        return lax.cond(
-            local_start <= positions[-1],
-            partial(
-                absorb,
-                queries=queries,
-                positions=positions,
-                key_block=block[:, :HEAD_SIZE],
-                value_block=block[:, HEAD_SIZE:],
-                key_start=local_start,
-            ),
-            lambda states: states,
-            states,
-        )
-
-    maxima, totals, summed = lax.fori_loop(0, piece_rows // block_rows, one_block, initial)
-    normalized = (summed / totals[:, :, None]).transpose(1, 0, 2)
-    attended = normalized.reshape(tok_rows, query_width).astype(jnp.bfloat16)
-    reduced_out_rows = lax.dot_general(
-        attended, out_down, (((1,), (1,)), ((), ())), preferred_element_type=jnp.float32
-    ).astype(jnp.bfloat16)
     out_rows = jnp.dot(reduced_out_rows, out_up, preferred_element_type=jnp.float32).astype(
         jnp.bfloat16
     )

time: 204 us -> 114 us (0.56)
  waiting for transfers between devices: 36.1 us -> 0 us
  Pallas kernels: 120 us -> 106 us
  between operations: 14.8 us -> 1.35 us
  matrix products: 15.3 us -> 3.23 us
  local copies, waits for them, and re-layouts: 8.81 us -> 2.5 us
  other arithmetic: 4.34 us -> 0.43 us
  loops' own time: 2.96 us -> 0 us
    pallas_call x1, Pallas kernels: 120 us -> 84 us  [shards(): pl.pallas_call(partial(fetch_kernel, seq_size, slots), out_shape=(jax.Sha...]
    all_gather x1 -> x0, waiting for transfers between devices: 36.1 us -> none  [shards(): lax.all_gather(jnp.concatenate([key_rows, value_rows], 1), 'seq', axis=0,...]
    pallas_call x0 -> x1, Pallas kernels: none -> 22.3 us  [shards(): pl.pallas_call(partial(attend_kernel, seq_size), out_shape=(jax.ShapeDtyp...]
    dot_general x11 -> x0, matrix products: 13 us -> none  [the longest x4 6.98 us: absorb(): jnp.einsum('hqk,kd->hqd', weights.astype(jnp.bfloat16), value_block, pref...]
    unnamed x18 -> x7, local copies, waits for them, and re-layouts: 6.09 us -> 2.5 us
    another operation x5 -> x0, loops' own time: 2.96 us -> none  [the longest x1 2.65 us: shards(): lax.fori_loop(0, piece_rows // block_rows, one_block, initial)]
    slice x6 -> x0, local copies, waits for them, and re-layouts: 2.67 us -> none  [the longest x4 2.46 us: one_block(): positions[-1]]
    reduce_sum x4 -> x0, other arithmetic: 2.05 us -> none  [absorb(): totals = totals * rescale + jnp.sum(weights, -1)]
  transfers between devices with their start and end apart: 1 -> 0, of which waited for: 1 -> 0; matrix products, arithmetic and copies ran while one was open for 0% -> 0% of each run, Pallas kernels for 0% -> 0%
where the time goes in v2:
time: 114 us
  Pallas kernels  106 us (93%)
  matrix products  3.23 us (3%)
  local copies, waits for them, and re-layouts  2.5 us (2%)
  between operations  1.35 us (1%)
    pallas_call x1, Pallas kernels, shards(): pl.pallas_call(partial(fetch_kernel, seq_size, slots), out_shape=(jax.Sha...  84 us
    pallas_call x1, Pallas kernels, shards(): pl.pallas_call(partial(attend_kernel, seq_size), out_shape=(jax.ShapeDtyp...  22.3 us
    dot_general x1, matrix products, shards(): jnp.dot(reduced_out_rows, out_up, preferred_element_type=jnp.float32)  3.23 us
    unnamed x7, local copies, waits for them, and re-layouts  2.5 us

profile of v2, /device:TPU:27, one launch (start us, length us, event | category | flops | bytes accessed | tf_op | source)
XLA Modules:
  0.0 113.8 jit_solution(18203147746215792379)
XLA Ops:
  1.3 0.3 fusion
  1.6 0.1 pad_maximum_fusion
  1.7 0.0 copy-start
  1.7 84.0 %fetch.1 = (bf16[128,192]{1,0:T(8,128)(2,1)}, bf16[64,2304]{1,0:T(8,128)(2,1)}, bf16[64,8192]{1,0:T(8,128)(2,1)}) custom-call(s32[2]{0:T(128)} %ids_ref.1, s32[16]{0:T(128)} %holder_ref.1, s32[1]{0:T(128)S(6)} %copy.12.entry_ref, bf16[128,8192]{1,0:T(8,128)(2,1)} %x_ref.1, bf16[1,192,8192]{2,1,0:T(8,128)(2,1)} %down_ref.1, bf16[1,64,1280]{2,1,0:T(8,128)(2,1)} %up_ref.1, ...), custom_call_target="tpu_custom_call" | custom-call | tf_op jit(solution)/shard_map/fetch/pallas_call | solution.py:570
  85.7 0.0 copy-done
  85.7 0.0 copy-start.1
  85.7 1.0 copy-done.1
  86.7 0.0 copy-start.2
  86.7 0.8 copy-done.2
  87.5 22.3 %attend.1 = (bf16[128,1024]{1,0:T(8,128)(2,1)S(1)}, bf16[128,64]{1,0:T(8,128)(2,1)S(1)}) custom-call(bf16[128,192]{1,0:T(8,128)(2,1)S(1)} %copy-done.2, bf16[64,2304]{1,0:T(8,128)(2,1)S(1)} %copy-done.1, bf16[128,1280]{1,0:T(8,128)(2,1)S(1)} %copy-done, f32[128,128]{1,0:T(8,128)S(1)} %get-tuple-element.15.cosine_ref, f32[128,128]{1,0:T(8,128)S(1)} %get-tuple-element.16.sine_ref), custom_call_target="tpu_custom_call" | custom-call | tf_op jit(solution)/shard_map/attend/pallas_call | solution.py:612
  109.9 3.2 %convolution_convert_fusion = bf16[128,8192]{1,0:T(8,128)(2,1)} fusion(bf16[128,64]{1,0:T(8,128)(2,1)S(1)} %get-tuple-element.10, bf16[64,8192]{1,0:T(8,128)(2,1)} %get-tuple-element.11), kind=kOutput, calls=%fused_computation | convolution fusion | flops 135266304 | bytes 3162112 | tf_op jit(solution)/shard_map/dot_general | solution.py:642
  113.1 0.7 copy.13
  (2 shorter events, 0.0 us)
Async XLA Ops:
  1.7 84.0 %copy-start = (bf16[128,1280]{1,0:T(8,128)(2,1)S(1)}, bf16[128,1280]{1,0:T(8,128)(2,1)}, u32[]{:S(2)}) copy-start(bf16[128,1280]{1,0:T(8,128)(2,1)} %base_ref.1) | copy-start | bytes 983044
  85.7 1.0 copy-start.1
  86.7 0.8 copy-start.2

commit v3 on v2

--- a/solution.py
+++ b/solution.py
@@ -87,6 +87,7 @@
     mate_rows,
     moving,
     whole,
+    x_rows,
     load_sem,
     mate_send,
     mate_recv,
@@ -138,6 +139,8 @@
     ]
     for load in loads:
         load.start()
+    x_load = pltpu.make_async_copy(x_ref, x_rows, load_sem.at[len(loads)])
+    x_load.start()
     for q in range(4):
         own[pl.ds(QUARTER * q + 64, 16), pl.ds(2304, 1792)] = jnp.zeros((16, 1792), jnp.bfloat16)
 
@@ -294,6 +297,7 @@
     for i in range(2):
         drain(cross, cross_recv.at[i])
 
+    x_load.wait()
     total = jnp.zeros((x_ref.shape[0], 3 * ADAPTER_RANK), jnp.float32)
 
     def shrink(block, total):
@@ -307,7 +311,7 @@
             for q in range(3)
         ]
         return total + lax.dot_general(
-            x_ref[:, at],
+            x_rows[:, at],
             jnp.concatenate(parts, 0),
             (((1,), (1,)), ((), ())),
             preferred_element_type=jnp.float32,
@@ -372,8 +376,7 @@
     totals,
     summed,
     line_send,
-    cross_send,
-    mate_send,
+    level_send,
     recv,
 ):
     columns, rows = chip_grid(seq_size // 2)
@@ -382,10 +385,10 @@
     core = me % 2
     x = (me // 2) % columns
     z = me // (2 * columns)
-    mate = me + 1 - 2 * core
+    peers = 2 * columns
     tokens = base_ref.shape[0]
     query_width = QUERY_PER_GROUP * HEAD_SIZE
-    level = 2 * columns * tokens
+    level = peers * tokens
 
     def device(z, x, core):
         return (z * columns + x) * 2 + core
@@ -400,9 +403,8 @@
         return carry
 
     lax.fori_loop(1, rows, greet_line, 0)
-    for i in range(1, columns):
-        greet(device(z, (x + i) % columns, core))
-    greet(mate)
+    for i in range(1, peers):
+        greet(z * peers + (me + i) % peers)
 
     rank = ADAPTER_RANK
 
@@ -428,7 +430,7 @@
         query_width + HEAD_SIZE, HEAD_SIZE, 2
     ).astype(jnp.bfloat16)
 
-    pl.semaphore_wait(barrier, rows - 1 + columns - 1 + 1)
+    pl.semaphore_wait(barrier, rows - 1 + peers - 1)
 
     def send(owner, target, send_sem):
         return pltpu.make_async_remote_copy(
@@ -443,32 +445,27 @@
     def to_line(later):
         return send(me, device(later, x, core), line_send.at[later])
 
-    def to_row(deep, i):
+    def to_peer(deep, i):
         return send(
             device(deep, x, core),
-            device(z, (x + i) % columns, core),
-            cross_send.at[deep * columns + i],
-        )
-
-    def to_mate(deep, i):
-        i = (x + i) % columns
-        return send(device(deep, i, core), mate, mate_send.at[deep * columns + i])
+            z * peers + (me + i) % peers,
+            level_send.at[deep * peers + i],
+        )
 
     def await_pair(owner):
         piece = pairs.at[rows_of(owner)]
         pltpu.make_async_copy(piece, piece, recv.at[owner]).wait()
 
     def relay(deep):
-        for i in range(1, columns):
-            to_row(deep, i).start()
-        to_mate(deep, 0).start()
+        for i in range(1, peers):
+            to_peer(deep, i).start()
 
     def start_line(later, carry):
         to_line(later).start()
         return carry
 
+    lax.fori_loop(z + 1, rows, start_line, 0)
     relay(z)
-    lax.fori_loop(z + 1, rows, start_line, 0)
 
     for h in range(QUERY_PER_GROUP):
         queries[pl.ds(h * tokens, tokens), :] = turn(project(h * HEAD_SIZE, HEAD_SIZE, 0))
@@ -486,11 +483,8 @@
             await_pair(device(deep - 1, x, core))
             relay(deep - 1)
 
-        for i in range(1, columns):
-            await_pair(device(deep, (x + i) % columns, core))
-            to_mate(deep, i).start()
-        for i in range(columns):
-            await_pair(device(deep, i, 1 - core))
+        for i in range(1, peers):
+            await_pair(deep * peers + (me + i) % peers)
 
         at = pl.ds(pl.multiple_of(deep * level, level), level)
         keys = pairs[at, pl.ds(0, HEAD_SIZE)]
@@ -539,10 +533,8 @@
     lax.fori_loop(z + 1, rows, end_line, 0)
 
     def end_level(deep, carry):
-        for i in range(1, columns):
-            to_row(deep, i).wait_send()
-        for i in range(columns):
-            to_mate(deep, i).wait_send()
+        for i in range(1, peers):
+            to_peer(deep, i).wait_send()
         return carry
 
     lax.fori_loop(0, z + 1, end_level, 0)
@@ -574,14 +566,15 @@
             jax.ShapeDtypeStruct((ADAPTER_RANK, 2304), bf16),
             jax.ShapeDtypeStruct((ADAPTER_RANK, width), bf16),
         ),
-        in_specs=[in_smem] * 3 + [in_vmem] + [in_any] * 4,
+        in_specs=[in_smem] * 3 + [in_any] * 5,
         out_specs=(in_vmem, in_vmem, in_vmem),
         scratch_shapes=[
             pltpu.VMEM((4 * QUARTER, width), bf16),
             pltpu.VMEM((2 * QUARTER, width), bf16),
             pltpu.VMEM((2, 2, LANE_ROWS * ALL_CHUNKS, BLOCK), bf16),
             pltpu.VMEM((8 * QUARTER, width), bf16),
-            pltpu.SemaphoreType.DMA((12,)),
+            pltpu.VMEM((tok_rows, width), bf16),
+            pltpu.SemaphoreType.DMA((13,)),
             pltpu.SemaphoreType.DMA,
             pltpu.SemaphoreType.DMA((10,)),
             pltpu.SemaphoreType.DMA((4,)),
@@ -624,8 +617,7 @@
             pltpu.VMEM((heads, 1), jnp.float32),
             pltpu.VMEM((heads, HEAD_SIZE), jnp.float32),
             pltpu.SemaphoreType.DMA((rows,)),
-            pltpu.SemaphoreType.DMA((rows * columns,)),
-            pltpu.SemaphoreType.DMA((rows * columns,)),
+            pltpu.SemaphoreType.DMA((seq_size,)),
             pltpu.SemaphoreType.DMA((seq_size,)),
         ],
         compiler_params=pltpu.CompilerParams(

time: 114 us -> 113 us (level)
  no operation moved by 1% of the time
where the time goes in v3:
time: 113 us
  Pallas kernels  105 us (93%)
  matrix products  3.24 us (3%)
  local copies, waits for them, and re-layouts  2.5 us (2%)
  between operations  1.35 us (1%)
    pallas_call x1, Pallas kernels, shards(): pl.pallas_call(partial(fetch_kernel, seq_size, slots), out_shape=(jax.Sha...  83.2 us
    pallas_call x1, Pallas kernels, shards(): pl.pallas_call(partial(attend_kernel, seq_size), out_shape=(jax.ShapeDtyp...  21.9 us
    dot_general x1, matrix products, shards(): jnp.dot(reduced_out_rows, out_up, preferred_element_type=jnp.float32)  3.24 us
    unnamed x7, local copies, waits for them, and re-layouts  2.5 us

profile of v3, /device:TPU:27, one launch (start us, length us, event | category | flops | bytes accessed | tf_op | source)
XLA Modules:
  0.0 112.6 jit_solution(4641857276101026219)
XLA Ops:
  1.3 0.3 fusion
  1.6 0.1 pad_maximum_fusion
  1.7 0.0 copy-start
  1.7 83.2 %fetch.1 = (bf16[128,192]{1,0:T(8,128)(2,1)}, bf16[64,2304]{1,0:T(8,128)(2,1)}, bf16[64,8192]{1,0:T(8,128)(2,1)}) custom-call(s32[2]{0:T(128)} %ids_ref.1, s32[16]{0:T(128)} %holder_ref.1, s32[1]{0:T(128)S(6)} %copy.12.entry_ref, bf16[128,8192]{1,0:T(8,128)(2,1)} %x_ref.1, bf16[1,192,8192]{2,1,0:T(8,128)(2,1)} %down_ref.1, bf16[1,64,1280]{2,1,0:T(8,128)(2,1)} %up_ref.1, ...), custom_call_target="tpu_custom_call" | custom-call | tf_op jit(solution)/shard_map/fetch/pallas_call | solution.py:562
  84.9 0.0 copy-done
  84.9 0.0 copy-start.1
  84.9 1.0 copy-done.1
  85.9 0.0 copy-start.2
  85.9 0.8 copy-done.2
  86.7 21.9 %attend.1 = (bf16[128,1024]{1,0:T(8,128)(2,1)S(1)}, bf16[128,64]{1,0:T(8,128)(2,1)S(1)}) custom-call(bf16[128,192]{1,0:T(8,128)(2,1)S(1)} %copy-done.2, bf16[64,2304]{1,0:T(8,128)(2,1)S(1)} %copy-done.1, bf16[128,1280]{1,0:T(8,128)(2,1)S(1)} %copy-done, f32[128,128]{1,0:T(8,128)S(1)} %get-tuple-element.15.cosine_ref, f32[128,128]{1,0:T(8,128)S(1)} %get-tuple-element.16.sine_ref), custom_call_target="tpu_custom_call" | custom-call | tf_op jit(solution)/shard_map/attend/pallas_call | solution.py:605
  108.7 3.2 %convolution_convert_fusion = bf16[128,8192]{1,0:T(8,128)(2,1)} fusion(bf16[128,64]{1,0:T(8,128)(2,1)S(1)} %get-tuple-element.10, bf16[64,8192]{1,0:T(8,128)(2,1)} %get-tuple-element.11), kind=kOutput, calls=%fused_computation | convolution fusion | flops 135266304 | bytes 3162112 | tf_op jit(solution)/shard_map/dot_general | solution.py:634
  111.9 0.7 copy.13
  (2 shorter events, 0.0 us)
Async XLA Ops:
  1.7 83.2 %copy-start = (bf16[128,1280]{1,0:T(8,128)(2,1)S(1)}, bf16[128,1280]{1,0:T(8,128)(2,1)}, u32[]{:S(2)}) copy-start(bf16[128,1280]{1,0:T(8,128)(2,1)} %base_ref.1) | copy-start | bytes 983044
  84.9 1.0 copy-start.1
  85.9 0.8 copy-start.2
